TPU v7x, 256 devices: a whole 4x4x8 slice. The times are simulated.
256 devices in a mesh: section: 32 (over z, y_lo, core), dp: 8 (over x, y_hi).
Axes of the slice: x: 4, y: 4 (y_hi: 2, y_lo: 2; y = y_hi * 2 + y_lo), z: 8, core: 2. Of those that a mesh axis runs over, the one named last changes fastest.
Arguments:
- inputs: bfloat16 [1024, 2560], P('dp'), may hold values from -6 to 6
- cotangent: bfloat16 [1024, 2560], P('dp'), may hold values from -6 to 6
- weights: bfloat16 [32, 2560, 2560], P('section', 'dp'), may hold values from -0.125 to 0.125
- adam_m: float32 [32, 2560, 2560], P('section', 'dp'), may hold values from -0.0064 to 0.0064
- adam_v: float32 [32, 2560, 2560], P('section', 'dp'), may hold values from 5e-06 to 6e-05
Outputs:
- update: bfloat16 [32, 2560, 2560], P('section', 'dp')
- shadow_weights: bfloat16 [32, 2560, 2560], P('section', 'dp')
- shadow_acts: bfloat16 [32, 1024, 2560], P('section', 'dp')
All inputs are finite; a program needn't handle non-finite values.
Results may differ from a plain program's by a relative error of at most 0.03.
Values may be sent and summed in bfloat16 or wider, within the bound.
A program may use at most 128 MiB of HBM per device.

v0:
```python
import jax
import jax.numpy as jnp
from jax import lax
from jax.sharding import PartitionSpec as P

MICRO = 8


branch_scale = 0.5
norm_eps = 1e-05
beta_one = 0.9
beta_two = 0.95
adam_eps = 1e-08
learn_rate = 0.01
step_count = 4.0
tanh_coef = 0.7978845608028654
cubic_coef = 0.044715


def from_behind(value, axis, steps):
    count = lax.axis_size(axis)
    initial, last = (max(0, -steps), min(count, count - steps))
    return lax.ppermute(value, axis, [(source, source + steps) for source in range(initial, last)])


def from_behind_2(shard, axis, by):
    peers = lax.axis_size(axis)
    return lax.ppermute(shard, axis, [(i, (i + by) % peers) for i in range(peers)])


def gelu_value(values):
    tanh_part = jnp.tanh(tanh_coef * (values + cubic_coef * values * values * values))
    return 0.5 * values * (1.0 + tanh_part)


def gelu_slope(values):
    tanh_part = jnp.tanh(tanh_coef * (values + cubic_coef * values * values * values))
    return 0.5 * (1.0 + tanh_part) + 0.5 * values * (1.0 - tanh_part * tanh_part) * tanh_coef * (
        1.0 + 3.0 * cubic_coef * values * values
    )


def normalize(current):
    as_float = current.astype(jnp.float32)
    inv_rms = lax.rsqrt(jnp.mean(as_float * as_float, axis=-1, keepdims=True) + norm_eps)
    return (as_float, inv_rms, as_float * inv_rms)


def adam_step(weight, moment_one, moment_two, gradient):
    moment_one = beta_one * moment_one + (1.0 - beta_one) * gradient
    moment_two = beta_two * moment_two + (1.0 - beta_two) * gradient * gradient
    corrected_one = moment_one / (1.0 - beta_one**step_count)
    corrected_two = moment_two / (1.0 - beta_two**step_count)
    direction = corrected_one / (jnp.sqrt(corrected_two) + adam_eps)
    new_weight = (weight.astype(jnp.float32) - learn_rate * direction).astype(jnp.bfloat16)
    return (direction.astype(jnp.bfloat16), new_weight)


def keep_slot(buffer, fresh_value, position, active):
    previous = lax.dynamic_index_in_dim(buffer, position, 0, keepdims=False)
    return lax.dynamic_update_index_in_dim(
        buffer, jnp.where(active, fresh_value, previous), position, 0
    )


def exchange_units(saved_inputs):
    flattened = saved_inputs.reshape(-1, saved_inputs.shape[-1])
    normed_low = normalize(flattened)[2].astype(jnp.bfloat16)
    return lax.all_to_all(normed_low, "dp", split_axis=1, concat_axis=0, tiled=True)


def on_device(inputs, cotangent, weights, adam_m, adam_v):
    sections = lax.axis_size("section")
    my_section = lax.axis_index("section")
    feature_count = inputs.shape[1]
    micro_count = MICRO
    block_rows = inputs.shape[0] // micro_count
    block_shape = (block_rows, feature_count)
    last_tick = sections + micro_count - 2
    full_weight = lax.all_gather(weights[0], "dp", axis=0, tiled=True)
    input_blocks = inputs.reshape(micro_count, block_rows, feature_count)
    target_blocks = cotangent.reshape(micro_count, block_rows, feature_count)

    def run_layer(current):
        as_float, inv_rms, normed = normalize(current)
        pre_act = jnp.dot(
            normed.astype(jnp.bfloat16), full_weight, preferred_element_type=jnp.float32
        )
        return ((as_float + branch_scale * gelu_value(pre_act)).astype(jnp.bfloat16), pre_act)

    def skip_layer(current):
        return (current, jnp.zeros(block_shape, jnp.float32))

    def forward_compute(clock_tick, incoming, saved_inputs, saved_outputs, saved_pre):
        slot_index = clock_tick - my_section
        active = jnp.logical_and(slot_index >= 0, slot_index < micro_count)
        position = jnp.clip(slot_index, 0, micro_count - 1)
        source_block = lax.dynamic_index_in_dim(input_blocks, position, 0, keepdims=False)
        current = jnp.where(my_section == 0, source_block, incoming)
        output, pre_act = lax.cond(active, run_layer, skip_layer, current)
        saved_inputs = keep_slot(saved_inputs, current, position, active)
        saved_outputs = keep_slot(saved_outputs, output, position, active)
        saved_pre = keep_slot(saved_pre, pre_act, position, active)
        return (output, saved_inputs, saved_outputs, saved_pre)

    def forward_tick(clock_tick, loop_state):
        incoming, saved_inputs, saved_outputs, saved_pre = loop_state
        output, saved_inputs, saved_outputs, saved_pre = forward_compute(
            clock_tick, incoming, saved_inputs, saved_outputs, saved_pre
        )
        outgoing = from_behind(output, "section", 1)
        return (outgoing, saved_inputs, saved_outputs, saved_pre)

    pre_start = jnp.zeros((micro_count, block_rows, feature_count), jnp.float32)
    empty_blocks = jnp.zeros((micro_count, block_rows, feature_count), jnp.bfloat16)
    forward_start = (jnp.zeros(block_shape, jnp.bfloat16), empty_blocks, empty_blocks, pre_start)
    incoming, saved_inputs, saved_outputs, saved_pre = lax.fori_loop(
        0, last_tick, forward_tick, forward_start
    )
    unused, saved_inputs, saved_outputs, saved_pre = forward_compute(
        last_tick, incoming, saved_inputs, saved_outputs, saved_pre
    )

    def run_back(grad_out, current, pre_act):
        as_float, inv_rms, normed = normalize(current)
        grad_float = grad_out.astype(jnp.float32)
        grad_pre = (grad_float * branch_scale * gelu_slope(pre_act)).astype(jnp.bfloat16)
        grad_normed = lax.dot_general(
            grad_pre, full_weight, (((1,), (1,)), ((), ())), preferred_element_type=jnp.float32
        )
        grad_in = grad_float + inv_rms * (
            grad_normed - normed * jnp.mean(grad_normed * normed, axis=-1, keepdims=True)
        )
        return (grad_in.astype(jnp.bfloat16), grad_pre)

    def skip_back(grad_out, current, pre_act):
        return (grad_out, jnp.zeros(block_shape, jnp.bfloat16))

    def backward_compute(clock_tick, incoming, saved_grads):
        slot_index = clock_tick - (sections - 1 - my_section)
        active = jnp.logical_and(slot_index >= 0, slot_index < micro_count)
        position = jnp.clip(slot_index, 0, micro_count - 1)
        source_block = lax.dynamic_index_in_dim(target_blocks, position, 0, keepdims=False)
        grad_out = jnp.where(my_section == sections - 1, source_block, incoming)
        current = lax.dynamic_index_in_dim(saved_inputs, position, 0, keepdims=False)
        pre_act = lax.dynamic_index_in_dim(saved_pre, position, 0, keepdims=False)
        grad_in, grad_pre = lax.cond(active, run_back, skip_back, grad_out, current, pre_act)
        saved_grads = keep_slot(saved_grads, grad_pre, position, active)
        return (grad_in, saved_grads)

    def backward_tick(clock_tick, loop_state):
        incoming, saved_grads = loop_state
        grad_in, saved_grads = backward_compute(clock_tick, incoming, saved_grads)
        outgoing = from_behind(grad_in, "section", -1)
        return (outgoing, saved_grads)

    backward_start = (jnp.zeros(block_shape, jnp.bfloat16), empty_blocks)
    incoming_grad, saved_grads = lax.fori_loop(0, last_tick, backward_tick, backward_start)
    unused_grad, saved_grads = backward_compute(last_tick, incoming_grad, saved_grads)
    unit_rows = exchange_units(saved_inputs)
    gathered_pre = lax.all_gather(saved_grads.reshape(-1, feature_count), "dp", axis=0, tiled=True)
    gradient = (
        lax.dot_general(
            unit_rows, gathered_pre, (((0,), (0,)), ((), ())), preferred_element_type=jnp.float32
        )
        / gathered_pre.shape[0]
    )
    direction, new_weight = adam_step(weights[0], adam_m[0], adam_v[0], gradient)
    shadow_weight, shadow_output = from_behind_2(
        (new_weight, saved_outputs.reshape(-1, feature_count)), "section", -1
    )
    return (direction[None], shadow_weight[None], shadow_output[None])


def solution(mesh):
    in_specs = (
        P("dp", None),
        P("dp", None),
        P("section", "dp", None),
        P("section", "dp", None),
        P("section", "dp", None),
    )
    out_specs = (P("section", "dp", None), P("section", "dp", None), P("section", "dp", None))
    return jax.shard_map(
        on_device, mesh=mesh, in_specs=in_specs, out_specs=out_specs, check_vma=False
    )
```

profile of v0, /device:TPU:4, one launch (start us, length us, event | category | flops | bytes accessed | tf_op | source)
XLA Modules:
  0.0 1350.4 jit_solution(14538219750988925066)
XLA Ops:
  8.0 161.5 %all-gather.6.cloned.1.call-done = bf16[1,2560,2560]{2,1,0:T(8,128)(2,1)} async-done(((bf16[1,320,2560]{2,1,0:T(8,128)(2,1)}), bf16[1,2560,2560]{2,1,0:T(8,128)(2,1)}) %all-gather.6.cloned.1.call-update) | async-done | bytes 13107216 | tf_op jit(solution)/shard_map/all_gather | solution.py:80
  169.7 364.6 %while.37 = (s32[]{:T(128)}, bf16[16,2560]{1,0:T(8,128)(2,1)S(1)}, bf16[8,16,2560]{2,1,0:T(8,128)(2,1)S(1)}, bf16[8,16,2560]{2,1,0:T(8,128)(2,1)S(1)}, f32[8,16,...) while((s32[]{:T(128)}, bf16[16,2560]{1,0:T(8,128)(2,1)S(1)}, ...), condition=%wide.region_4.5_spmd, body=%wide.region_0.4_spmd.sunk | while | flops 210616352 | bytes 15647255 | solution.py:117
  269.9 11.6 collective-permute-start
  290.1 11.6 collective-permute-start
  310.3 9.1 collective-permute-start
  328.9 12.5 collective-permute-start
  366.2 7.7 collective-permute-start
  398.7 8.6 collective-permute-start
  432.2 7.7 collective-permute-start
  464.7 8.6 collective-permute-start
  515.3 9.1 collective-permute-start
  535.5 684.4 %while.38 = (s32[]{:T(128)}, bf16[16,2560]{1,0:T(8,128)(2,1)S(1)}, bf16[8,16,2560]{2,1,0:T(8,128)(2,1)S(1)}, s32[]{:T(128)}, pred[]{:T(512)}, /*index=5*/bf16[8,...) while((s32[]{:T(128)}, bf16[16,2560]{1,0:T(8,128)(2,1)S(1)}, ...), condition=%wide.region_14.15_spmd, body=%wide.region_9.14_spmd.sunk | while | flops 211271712 | bytes 15238005 | solution.py:158
  538.4 13.1 collective-permute-done.1
  831.6 260.8 %collective-permute-done.1 = bf16[16,2560]{1,0:T(8,128)(2,1)S(1)} collective-permute-done((bf16[16,2560]{1,0:T(8,128)(2,1)S(1)}, bf16[16,2560]{1,0:T(8,128)(2,1)S(1)}, u32[]{:S(2)}, u32[]{:S(2)}) %collective-permute-start.1) | collective-permute-done | bytes 81952 | tf_op jit(solution)/shard_map/while/body/eval_jaxpr/ppermute | solution.py:23
  1093.3 9.4 conditional.9
  1094.3 8.4 fusion.24
  1111.5 9.4 conditional.9
  1112.5 8.4 fusion.24
  1129.7 9.4 conditional.9
  1130.7 8.4 fusion.24
  1147.9 9.4 conditional.9
  1148.9 8.4 fusion.24
  1166.1 9.4 conditional.9
  1167.1 8.4 fusion.24
  1184.3 9.4 conditional.9
  1185.3 8.4 fusion.24
  1202.5 9.4 conditional.9
  1203.5 8.4 fusion.24
  1223.4 13.3 all_to_all.16
  1236.6 67.8 %all-gather.4.cloned.1.call-done = bf16[1024,2560]{1,0:T(8,128)(2,1)} async-done(((bf16[128,2560]{1,0:T(8,128)(2,1)}), bf16[1024,2560]{1,0:T(8,128)(2,1)}) %all-gather.4.cloned.1.call-update) | async-done | bytes 5242896 | tf_op jit(solution)/shard_map/all_gather | solution.py:161
  1304.4 9.1 fusion.47
  1317.1 24.4 %collective-permute-done.3 = bf16[128,2560]{1,0:T(8,128)(2,1)S(1)} collective-permute-done((bf16[128,2560]{1,0:T(8,128)(2,1)S(1)}, bf16[128,2560]{1,0:T(8,128)(2,1)S(1)}, u32[]{:S(2)}, u32[]{:S(2)}) %collective-permute-start.3) | collective-permute-done | bytes 655392 | tf_op jit(solution)/shard_map/ppermute | solution.py:28
  (734 shorter events, 713.5 us)
Async XLA Ops:
  7.2 162.3 %all-gather.6.cloned.1.call-start = ((), (), s32[]{:S(2)}) async-start(), calls=%async_computation.2 | async-start | bytes 14745600 | tf_op jit(solution)/shard_map/all_gather | solution.py:80
  7.9 1296.5 %all-gather.4.cloned.1.call-start = ((), (), s32[]{:S(2)}) async-start(), calls=%async_computation.1 | async-start | bytes 5898240 | tf_op jit(solution)/shard_map/all_gather | solution.py:161
  269.9 12.5 collective-permute-start
  290.1 12.5 collective-permute-start
  310.3 10.0 collective-permute-start
  328.9 13.4 collective-permute-start
  366.2 8.6 collective-permute-start
  398.7 9.5 collective-permute-start
  432.2 8.6 collective-permute-start
  464.7 9.5 collective-permute-start
  498.1 8.6 collective-permute-start
  515.3 10.0 collective-permute-start
  526.4 7.9 collective-permute-start
  537.1 14.4 %collective-permute-start.1 = (bf16[16,2560]{1,0:T(8,128)(2,1)S(1)}, bf16[16,2560]{1,0:T(8,128)(2,1)S(1)}, u32[]{:S(2)}, u32[]{:S(2)}) collective-permute-start(bf16[16,2560]{1,0:T(8,128)(2,1)S(1)} %get-tuple-element.675), channel_id=1, source_target_pairs={{8,0},{16,8},{24,16},{32,24},{40,32},{48,40},{56,48},{64,56},{72,6... | collective-permute-start | bytes 245768 | tf_op jit(solution)/shard_map/while/body/eval_jaxpr/ppermute | solution.py:23
  553.0 8.5 collective-permute-start.1
  572.4 8.5 collective-permute-start.1
  591.7 8.5 collective-permute-start.1
  611.0 8.5 collective-permute-start.1
  630.4 8.5 collective-permute-start.1
  649.7 8.5 collective-permute-start.1
  669.1 8.5 collective-permute-start.1
  688.4 8.5 collective-permute-start.1
  830.3 262.2 %collective-permute-start.1 = (bf16[16,2560]{1,0:T(8,128)(2,1)S(1)}, bf16[16,2560]{1,0:T(8,128)(2,1)S(1)}, u32[]{:S(2)}, u32[]{:S(2)}) collective-permute-start(bf16[16,2560]{1,0:T(8,128)(2,1)S(1)} %get-tuple-element.675), channel_id=1, source_target_pairs={{8,0},{16,8},{24,16},{32,24},{40,32},{48,40},{56,48},{64,56},{72,6... | collective-permute-start | bytes 245768 | tf_op jit(solution)/shard_map/while/body/eval_jaxpr/ppermute | solution.py:23
  1102.8 7.9 collective-permute-start.1
  1121.0 7.9 collective-permute-start.1
  1139.2 7.9 collective-permute-start.1
  1157.4 7.9 collective-permute-start.1
  1175.6 7.9 collective-permute-start.1
  1193.8 7.9 collective-permute-start.1
  1212.0 7.9 collective-permute-start.1
  1313.6 28.0 %collective-permute-start.2 = (bf16[320,2560]{1,0:T(8,128)(2,1)S(1)}, bf16[320,2560]{1,0:T(8,128)(2,1)S(1)}, u32[]{:S(2)}, u32[]{:S(2)}) collective-permute-start(bf16[320,2560]{1,0:T(8,128)(2,1)S(1)} %get-tuple-element.553), channel_id=1, source_target_pairs={{0,248},{8,0},{16,8},{24,16},{32,24},{40,32},{48,40},{56,48},{64,5... | collective-permute-start | bytes 4915208 | tf_op jit(solution)/shard_map/ppermute | solution.py:28
  1316.0 25.6 %collective-permute-start.3 = (bf16[128,2560]{1,0:T(8,128)(2,1)S(1)}, bf16[128,2560]{1,0:T(8,128)(2,1)S(1)}, u32[]{:S(2)}, u32[]{:S(2)}) collective-permute-start(bf16[128,2560]{1,0:T(8,128)(2,1)S(1)} %bitcast.158), channel_id=1, source_target_pairs={{0,248},{8,0},{16,8},{24,16},{32,24},{40,32},{48,40},{56,48},{64,5... | collective-permute-start | bytes 1966088 | tf_op jit(solution)/shard_map/ppermute | solution.py:28
  (51 other events, 407.5 us)
Sparse Core Ops, SparseCore 0:
  10.6 158.7 all-gather.5
  1221.9 82.4 all-gather.3
where the time goes:
time: 1360 us; the launch traced here: 1350 us
  waiting for transfers between devices  790 us (58%)
  starting transfers between devices  291 us (21%)
  matrix products  120 us (9%)
  other arithmetic  89.6 us (7%)
  local copies, waits for them, and re-layouts  27 us (2%)
  between operations  14.2 us (1%)
    ppermute x76, waiting for transfers between devices, from_behind(): lax.ppermute(value, axis, [(source, source + steps) for source in range(i...  535 us
    ppermute x76, starting transfers between devices, from_behind(): lax.ppermute(value, axis, [(source, source + steps) for source in range(i...  287 us
    all_gather x1, waiting for transfers between devices, on_device(): full_weight = lax.all_gather(weights[0], 'dp', axis=0, tiled=True)  161 us
    all_gather x1, waiting for transfers between devices, on_device(): lax.all_gather(saved_grads.reshape(-1, feature_count), 'dp', axis=0, tile...  67.8 us
    dot_general x7, matrix products, run_back(): lax.dot_general(grad_pre, full_weight, (((1,), (1,)), ((), ())), preferre...  58.6 us
    dot_general x8, matrix products, run_layer(): jnp.dot(normed.astype(jnp.bfloat16), full_weight, preferred_element_type=...  52.7 us
    dynamic_update_slice x156, other arithmetic, keep_slot(): lax.dynamic_update_index_in_dim(buffer, jnp.where(active, fresh_value, pr...  45.9 us
    select_n x38, other arithmetic, backward_compute(): grad_out = jnp.where(my_section == sections - 1, source_block, incoming)  34.1 us
  transfers between devices with their start and end apart: 80, of which 79 were waited for; matrix products, arithmetic and copies ran while one was open for 1% of the time, Pallas kernels for 0%

commit v1 on v0

v1 whole, which is shorter than its diff:
```python
import functools
import jax
import jax.numpy as jnp
from jax import lax
from jax.experimental import pallas as pl
from jax.experimental.pallas import tpu as pltpu
from jax.sharding import PartitionSpec as P

MICRO = 8
CHUNK = 256

branch_scale = 0.5
norm_eps = 1e-05
beta_one = 0.9
beta_two = 0.95
adam_eps = 1e-08
learn_rate = 0.01
step_count = 4.0
tanh_coef = 0.7978845608028654
cubic_coef = 0.044715


def adam_step(weight, moment_one, moment_two, gradient):
    moment_one = beta_one * moment_one + (1.0 - beta_one) * gradient
    moment_two = beta_two * moment_two + (1.0 - beta_two) * gradient * gradient
    corrected_one = moment_one / (1.0 - beta_one**step_count)
    corrected_two = moment_two / (1.0 - beta_two**step_count)
    direction = corrected_one / (jnp.sqrt(corrected_two) + adam_eps)
    new_weight = (weight.astype(jnp.float32) - learn_rate * direction).astype(jnp.bfloat16)
    return (direction.astype(jnp.bfloat16), new_weight)


def chain_kernel(
    sections,
    inputs_ref,
    cotangent_ref,
    weight_ref,
    normed_ref,
    grads_ref,
    shadow_ref,
    weight,
    flipped,
    arrived,
    outputs,
    grads_in,
    grads_out,
    pre_acts,
    slopes,
    scales,
    load_sem,
    ahead_send,
    ahead_recv,
    back_send,
    back_recv,
    shadow_send,
    shadow_recv,
):
    micro, rows, width = arrived.shape
    me = lax.axis_index("section")
    after = lax.rem(me + 1, sections)
    before = lax.rem(me + sections - 1, sections)

    load = pltpu.make_async_copy(weight_ref, weight, load_sem)
    load.start()
    barrier = pltpu.get_barrier_semaphore()
    for peer in (before, after):
        pl.semaphore_signal(barrier, inc=1, device_id={"section": peer})
    pl.semaphore_wait(barrier, 2)

    def ahead(i):
        return pltpu.make_async_remote_copy(
            src_ref=outputs.at[i],
            dst_ref=arrived.at[i],
            send_sem=ahead_send.at[i],
            recv_sem=ahead_recv.at[i],
            device_id={"section": after},
        )

    def back(i):
        return pltpu.make_async_remote_copy(
            src_ref=grads_out.at[i],
            dst_ref=grads_in.at[i],
            send_sem=back_send.at[i],
            recv_sem=back_recv.at[i],
            device_id={"section": before},
        )

    def shadow(i):
        return pltpu.make_async_remote_copy(
            src_ref=outputs.at[i],
            dst_ref=shadow_ref.at[i],
            send_sem=shadow_send.at[i],
            recv_sem=shadow_recv.at[i],
            device_id={"section": before},
        )

    def flip():
        blocks = width // CHUNK

        def one(k, carry):
            row = pl.multiple_of((k // blocks) * CHUNK, CHUNK)
            column = pl.multiple_of(lax.rem(k, blocks) * CHUNK, CHUNK)
            flipped[pl.ds(column, CHUNK), pl.ds(row, CHUNK)] = weight[
                pl.ds(row, CHUNK), pl.ds(column, CHUNK)
            ].T
            return carry

        lax.fori_loop(0, blocks * blocks, one, 0)

    load.wait()

    @pl.when(me == 0)
    def _():
        arrived[...] = inputs_ref[...]

    @pl.when(me == sections - 1)
    def _():
        grads_in[...] = cotangent_ref[...]

    @pl.when(me >= sections // 2)
    def _():
        flip()

    def forward(i, carry):
        @pl.when(me > 0)
        def _():
            ahead(i).wait_recv()

        current = arrived[i].astype(jnp.float32)
        scale = lax.rsqrt(jnp.mean(current * current, axis=-1, keepdims=True) + norm_eps)
        scales[i] = jnp.broadcast_to(scale, (rows, 128))
        normed = (current * scale).astype(jnp.bfloat16)
        normed_ref[i] = normed
        for at in range(0, width, CHUNK):
            part = pl.ds(at, CHUNK)
            v = jnp.dot(normed, weight[:, part], preferred_element_type=jnp.float32)
            t = jnp.tanh(tanh_coef * (v + cubic_coef * v * v * v))
            out = arrived[i, :, part].astype(jnp.float32) + branch_scale * (0.5 * v * (1.0 + t))
            outputs[i, :, part] = out.astype(jnp.bfloat16)
            pre_acts[i, :, part] = v
            slope = 0.5 * (1.0 + t) + 0.5 * v * (1.0 - t * t) * tanh_coef * (
                1.0 + 3.0 * cubic_coef * v * v
            )
            slopes[i, :, part] = branch_scale * slope

        @pl.when(me < sections - 1)
        def _():
            ahead(i).start()

        shadow(i).start()
        return carry

    lax.fori_loop(0, micro, forward, 0)

    @pl.when(me < sections // 2)
    def _():
        flip()

    def backward(i, carry):
        @pl.when(me < sections - 1)
        def _():
            back(i).wait_recv()

        grad = grads_in[i].astype(jnp.float32)
        grad_pre = (grad * slopes[i]).astype(jnp.bfloat16)
        grads_ref[i] = grad_pre

        @pl.when(me > 0)
        def _():
            overlap = jnp.sum(
                grad_pre.astype(jnp.float32) * pre_acts[i], axis=-1, keepdims=True
            ) * (1.0 / width)
            scale = scales[i][:, :1]
            pull = scale * scale * overlap
            for at in range(0, width, CHUNK):
                part = pl.ds(at, CHUNK)
                g = jnp.dot(grad_pre, flipped[:, part], preferred_element_type=jnp.float32)
                a = arrived[i, :, part].astype(jnp.float32)
                total = grads_in[i, :, part].astype(jnp.float32) + scale * g - pull * a
                grads_out[i, :, part] = total.astype(jnp.bfloat16)
            back(i).start()

        return carry

    lax.fori_loop(0, micro, backward, 0)

    def settle(i, carry):
        @pl.when(me < sections - 1)
        def _():
            ahead(i).wait_send()

        @pl.when(me > 0)
        def _():
            back(i).wait_send()

        shadow(i).wait_send()
        shadow(i).wait_recv()
        return carry

    lax.fori_loop(0, micro, settle, 0)


def chain(sections, inputs, cotangent, full_weight):
    tokens, width = inputs.shape
    rows = tokens // MICRO
    block = (MICRO, rows, width)
    low = jax.ShapeDtypeStruct(block, jnp.bfloat16)
    in_vmem = pl.BlockSpec(memory_space=pltpu.VMEM)
    anywhere = pl.BlockSpec(memory_space=pl.ANY)
    return pl.pallas_call(
        functools.partial(chain_kernel, sections),
        out_shape=(low, low, low),
        in_specs=[in_vmem, in_vmem, anywhere],
        out_specs=(in_vmem, in_vmem, anywhere),
        scratch_shapes=[
            pltpu.VMEM((width, width), jnp.bfloat16),
            pltpu.VMEM((width, width), jnp.bfloat16),
            pltpu.VMEM(block, jnp.bfloat16),
            pltpu.VMEM(block, jnp.bfloat16),
            pltpu.VMEM(block, jnp.bfloat16),
            pltpu.VMEM(block, jnp.bfloat16),
            pltpu.VMEM(block, jnp.float32),
            pltpu.VMEM(block, jnp.float32),
            pltpu.VMEM((MICRO, rows, 128), jnp.float32),
            pltpu.SemaphoreType.DMA,
        ]
        + [pltpu.SemaphoreType.DMA((MICRO,))] * 6,
        compiler_params=pltpu.CompilerParams(
            collective_id=0, has_side_effects=True, vmem_limit_bytes=56 * 2**20
        ),
        cost_estimate=pl.CostEstimate(
            flops=4 * tokens * width * width,
            bytes_accessed=2 * width * width,
            transcendentals=tokens * width,
        ),
    )(inputs.reshape(block), cotangent.reshape(block), full_weight)


def on_device(inputs, cotangent, weights, adam_m, adam_v):
    sections = lax.axis_size("section")
    tokens, width = inputs.shape
    full_weight = lax.all_gather(weights[0], "dp", axis=0, tiled=True)
    normed, grads, shadow_output = chain(sections, inputs, cotangent, full_weight)
    normed = normed.reshape(tokens, width)
    grads = grads.reshape(tokens, width)
    unit_rows = lax.all_to_all(normed, "dp", split_axis=1, concat_axis=0, tiled=True)
    gathered = lax.all_gather(grads, "dp", axis=0, tiled=True)
    gradient = (
        lax.dot_general(
            unit_rows, gathered, (((0,), (0,)), ((), ())), preferred_element_type=jnp.float32
        )
        / gathered.shape[0]
    )
    direction, new_weight = adam_step(weights[0], adam_m[0], adam_v[0], gradient)
    shift = [(i, (i - 1) % sections) for i in range(sections)]
    shadow_weight = lax.ppermute(new_weight, "section", shift)
    return (direction[None], shadow_weight[None], shadow_output.reshape(1, tokens, width))


def solution(mesh):
    in_specs = (
        P("dp", None),
        P("dp", None),
        P("section", "dp", None),
        P("section", "dp", None),
        P("section", "dp", None),
    )
    out_specs = (P("section", "dp", None), P("section", "dp", None), P("section", "dp", None))
    return jax.shard_map(
        on_device, mesh=mesh, in_specs=in_specs, out_specs=out_specs, check_vma=False
    )
```

time: 1360 us -> 573 us (0.42)
  waiting for transfers between devices: 790 us -> 235 us
  starting transfers between devices: 291 us -> 2.44 us
  Pallas kernels: 0 us -> 286 us
  matrix products: 120 us -> 8.39 us
  other arithmetic: 89.6 us -> 0 us
  local copies, waits for them, and re-layouts: 27 us -> 4.38 us
    ppermute x78 -> x1, waiting for transfers between devices: 560 us -> 18.6 us  [on_device(): shadow_weight = lax.ppermute(new_weight, 'section', shift)]
    ppermute x78 -> x1, starting transfers between devices: 291 us -> 2.37 us  [on_device(): shadow_weight = lax.ppermute(new_weight, 'section', shift)]
    pallas_call x0 -> x1, Pallas kernels: none -> 286 us  [chain(): pl.pallas_call(functools.partial(chain_kernel, sections), out_shape=(low,...]
    dot_general x16 -> x1, matrix products: 120 us -> 8.39 us  [on_device(): lax.dot_general(unit_rows, gathered, (((0,), (0,)), ((), ())), preferred_...]
    dynamic_update_slice x156 -> x0, other arithmetic: 45.9 us -> none  [keep_slot(): lax.dynamic_update_index_in_dim(buffer, jnp.where(active, fresh_value, pr...]
    select_n x38 -> x0, other arithmetic: 34.1 us -> none  [backward_compute(): grad_out = jnp.where(my_section == sections - 1, source_block, incoming)]
    another operation x64 -> x0, local copies, waits for them, and re-layouts: 20.4 us -> none
  transfers between devices with their start and end apart: 80 -> 3, of which waited for: 79 -> 3; matrix products, arithmetic and copies ran while one was open for 1% -> 0% of each run, Pallas kernels for 0% -> 0%
where the time goes in v1:
time: 573 us; the launch traced here: 572 us
  Pallas kernels  286 us (50%)
  waiting for transfers between devices  235 us (41%)
  blocking collectives  21.9 us (4%)
  between operations  14.1 us (2%)
  matrix products  8.39 us (1%)
    pallas_call x1, Pallas kernels, chain(): pl.pallas_call(functools.partial(chain_kernel, sections), out_shape=(low,...  286 us
    all_gather x1, waiting for transfers between devices, on_device(): full_weight = lax.all_gather(weights[0], 'dp', axis=0, tiled=True)  161 us
    all_gather x1, waiting for transfers between devices, on_device(): gathered = lax.all_gather(grads, 'dp', axis=0, tiled=True)  54.2 us
    all_to_all x1, blocking collectives, on_device(): lax.all_to_all(normed, 'dp', split_axis=1, concat_axis=0, tiled=True)  21.9 us
    ppermute x1, waiting for transfers between devices, on_device(): shadow_weight = lax.ppermute(new_weight, 'section', shift)  18.6 us
  transfers between devices with their start and end apart: 3, of which 3 were waited for; matrix products, arithmetic and copies ran while one was open for 0% of the time, Pallas kernels for 0%

profile of v1, /device:TPU:4, one launch (start us, length us, event | category | flops | bytes accessed | tf_op | source)
XLA Modules:
  0.0 571.8 jit_solution(18252859850716696606)
XLA Ops:
  7.2 0.0 all-gather.6.cloned.1.call-start
  7.2 0.7 all-gather.6.cloned.1.call-update
  7.9 0.0 all-gather.4.cloned.1.call-start
  7.9 161.5 %all-gather.6.cloned.1.call-done = bf16[1,2560,2560]{2,1,0:T(8,128)(2,1)} async-done(((bf16[1,320,2560]{2,1,0:T(8,128)(2,1)}), bf16[1,2560,2560]{2,1,0:T(8,128)(2,1)}) %all-gather.6.cloned.1.call-update) | async-done | bytes 13107216 | tf_op jit(solution)/shard_map/all_gather | solution.py:242
  169.4 285.5 %shard_map.76 = (bf16[8,16,2560]{2,1,0:T(8,128)(2,1)}, bf16[8,16,2560]{2,1,0:T(8,128)(2,1)}, bf16[8,16,2560]{2,1,0:T(8,128)(2,1)}) custom-call(bf16[8,16,2560]{2,1,0:T(8,128)(2,1)} %bitcast.46, bf16[8,16,2560]{2,1,0:T(8,128)(2,1)} %bitcast.47, bf16[2560,2560]{1,0:T(8,128)(2,1)} %bitcast.44), custom_call_target="tpu_custom_call" | custom-call | flops 3355443200 | bytes 13107200 | tf_op jit(solution)/shard_map/pallas_call | solution.py:210
  455.0 0.0 copy-start
  455.0 0.0 all-gather.4.cloned.1.call-update
  455.0 1.8 all_to_all.14
  456.9 0.5 copy.9
  457.4 21.9 %all_to_all.19 = bf16[128,8,320]{0,2,1:T(8,128)(2,1)S(1)} all-to-all(bf16[128,8,320]{0,2,1:T(8,128)(2,1)S(1)} %copy.9), channel_id=1, replica_groups=mesh['section'=32,'dp'=8] {'dp'}, dimensions={1} | all-to-all | bytes 1310720 | tf_op jit(solution)/shard_map/all_to_all | solution.py:246
  479.3 54.2 %all-gather.4.cloned.1.call-done = bf16[1024,2560]{1,0:T(8,128)(2,1)} async-done(((bf16[128,2560]{1,0:T(8,128)(2,1)}), bf16[1024,2560]{1,0:T(8,128)(2,1)}) %all-gather.4.cloned.1.call-update) | async-done | bytes 5242896 | tf_op jit(solution)/shard_map/all_gather | solution.py:247
  533.6 0.0 copy-done
  533.6 8.4 %fusion = (bf16[320,2560]{1,0:T(8,128)(2,1)S(1)}, bf16[1,320,2560]{2,1,0:T(8,128)(2,1)}) fusion(bf16[1,320,2560]{2,1,0:T(8,128)(2,1)S(1)} %copy-done, f32[1,320,2560]{2,1,0:T(8,128)} %param.9, bf16[1024,2560]{1,0:T(8,128)(2,1)} %all-gather.4.cloned.1.call-done, f32[1,320,2560]{2,1,0:T(8,128)} %param.8, bf16[128,8,320]{0,2,1:T(8,128)(2,1)S(1)} %all_to_all.19), kind=kOutput, calls=%fused_computation.1 | convolution fusion | flops 1691648000 | bytes 17367040 | tf_op jit(solution)/shard_map/dot_general | solution.py:249
  542.0 0.0 copy-start.1
  542.0 2.4 collective-permute-start
  544.3 18.6 %collective-permute-done = bf16[320,2560]{1,0:T(8,128)(2,1)S(1)} collective-permute-done((bf16[320,2560]{1,0:T(8,128)(2,1)S(1)}, bf16[320,2560]{1,0:T(8,128)(2,1)S(1)}, u32[]{:S(2)}, u32[]{:S(2)}) %collective-permute-start) | collective-permute-done | bytes 1638432 | tf_op jit(solution)/shard_map/ppermute | solution.py:256
  563.0 1.2 copy.20
  564.1 0.0 copy-done.1
  564.1 0.8 copy.21
Async XLA Ops:
  7.2 162.3 %all-gather.6.cloned.1.call-start = ((), (), s32[]{:S(2)}) async-start(), calls=%async_computation.2 | async-start | bytes 14745600 | tf_op jit(solution)/shard_map/all_gather | solution.py:242
  7.9 525.7 %all-gather.4.cloned.1.call-start = ((), (), s32[]{:S(2)}) async-start(), calls=%async_computation.1 | async-start | bytes 5898240 | tf_op jit(solution)/shard_map/all_gather | solution.py:247
  455.0 78.6 %copy-start = (bf16[1,320,2560]{2,1,0:T(8,128)(2,1)S(1)}, bf16[1,320,2560]{2,1,0:T(8,128)(2,1)}, u32[]{:S(2)}) copy-start(bf16[1,320,2560]{2,1,0:T(8,128)(2,1)} %param.7) | copy-start | bytes 4915204
  542.0 22.2 %copy-start.1 = (bf16[8,16,2560]{2,1,0:T(8,128)(2,1)S(1)}, bf16[8,16,2560]{2,1,0:T(8,128)(2,1)}, u32[]{:S(2)}) copy-start(bf16[8,16,2560]{2,1,0:T(8,128)(2,1)} %get-tuple-element.8) | copy-start | bytes 1966084
  542.0 21.0 %collective-permute-start = (bf16[320,2560]{1,0:T(8,128)(2,1)S(1)}, bf16[320,2560]{1,0:T(8,128)(2,1)S(1)}, u32[]{:S(2)}, u32[]{:S(2)}) collective-permute-start(bf16[320,2560]{1,0:T(8,128)(2,1)S(1)} %get-tuple-element.9), channel_id=1, source_target_pairs={{0,248},{8,0},{16,8},{24,16},{32,24},{40,32},{48,40},{56,48},{64,5... | collective-permute-start | bytes 4915208 | tf_op jit(solution)/shard_map/ppermute | solution.py:256
Sparse Core Ops, SparseCore 0:
  10.6 158.7 all-gather.5
  455.1 78.3 all-gather.3

commit v2 on v1

v2 whole, which is shorter than its diff:
```python
import functools
import jax
import jax.numpy as jnp
from jax import lax
from jax.experimental import pallas as pl
from jax.experimental.pallas import tpu as pltpu
from jax.sharding import PartitionSpec as P

MICRO = 8
CHUNK = 256
PIECES = 4
WINDOW = 384

branch_scale = 0.5
norm_eps = 1e-05
beta_one = 0.9
beta_two = 0.95
adam_eps = 1e-08
learn_rate = 0.01
step_count = 4.0
tanh_coef = 0.7978845608028654
cubic_coef = 0.044715


def chain_kernel(
    sections,
    replicas,
    inputs_ref,
    cotangent_ref,
    shard_ref,
    moment_one_ref,
    moment_two_ref,
    update_ref,
    shadow_weight_ref,
    shadow_ref,
    weight,
    flipped,
    arrived,
    outputs,
    grads_in,
    grads_out,
    pre_acts,
    slopes,
    scales,
    normed_all,
    units,
    units_flipped,
    gathered,
    moment_one,
    moment_two,
    fresh,
    stage,
    load_sem,
    ahead_send,
    ahead_recv,
    back_send,
    back_recv,
    shadow_send,
    shadow_recv,
    weight_send,
    weight_recv,
    grad_send,
    grad_recv,
    unit_send,
    unit_recv,
    fresh_send,
    fresh_recv,
):
    micro, rows, width = arrived.shape
    shard = width // replicas
    piece = shard // PIECES
    ring = replicas // 2
    tokens = micro * rows
    blocks = width // CHUNK
    me = lax.axis_index("section")
    mine = lax.axis_index("dp")
    after = lax.rem(me + 1, sections)
    before = lax.rem(me + sections - 1, sections)
    line, side = mine // 2, lax.rem(mine, 2)

    def peer(step, across=False):
        return lax.rem(line + step + ring, ring) * 2 + (1 - side if across else side)

    right, left, facing, far = peer(1), peer(-1), peer(0, True), peer(2)

    loads = [
        pltpu.make_async_copy(
            shard_ref,
            weight.at[pl.ds(pl.multiple_of(mine * shard, 16), shard)],
            load_sem.at[0],
        ),
        pltpu.make_async_copy(moment_one_ref, moment_one, load_sem.at[1]),
        pltpu.make_async_copy(moment_two_ref, moment_two, load_sem.at[2]),
    ]
    loads[0].start()
    barrier = pltpu.get_barrier_semaphore()
    for other in (before, after):
        pl.semaphore_signal(barrier, inc=1, device_id={"section": other})
    for step in range(1, replicas):
        pl.semaphore_signal(barrier, inc=1, device_id={"dp": lax.rem(mine + step, replicas)})
    pl.semaphore_wait(barrier, replicas + 1)

    def spread_over(place, own, sends, recvs):
        def move(lane, owner, i, to, source=None):
            return pltpu.make_async_remote_copy(
                src_ref=place(owner, i) if source is None else source,
                dst_ref=place(owner, i),
                send_sem=sends.at[lane, i],
                recv_sem=recvs.at[owner, i],
                device_id={"dp": to},
            )

        def landed(owner, i):
            move(0, owner, i, mine).wait_recv()

        def spread(i):
            for lane, to in enumerate((facing, right, left)):
                move(lane, mine, i, to, own(i)).start()

        def relay(i):
            turn = 2 * lax.rem(i, 2) - 1
            landed(peer(turn), i)
            move(3, peer(turn), i, peer(-turn)).start()
            landed(facing, i)
            move(4, facing, i, right).start()
            move(5, facing, i, left).start()

        def cross(i):
            landed(far, i)
            move(6, far, i, facing).start()

        def finish(i):
            turn = 2 * lax.rem(i, 2) - 1
            landed(peer(-turn), i)
            landed(peer(1, True), i)
            landed(peer(-1, True), i)
            landed(peer(2, True), i)
            for lane in range(7):
                move(lane, mine, i, mine).wait_send()

        return spread, relay, cross, finish

    def each(count, *steps):
        for step in steps:

            def one(i, carry, step=step):
                step(i)
                return carry

            lax.fori_loop(0, count, one, 0)

    def weight_place(owner, i):
        return weight.at[pl.ds(pl.multiple_of(owner * shard + i * piece, 16), piece)]

    weight_spread = spread_over(
        weight_place,
        lambda i: shard_ref.at[pl.ds(pl.multiple_of(i * piece, 16), piece)],
        weight_send,
        weight_recv,
    )
    grad_spread, grad_relay, grad_cross, grad_finish = spread_over(
        lambda owner, i: gathered.at[owner, i],
        lambda i: gathered.at[mine, i],
        grad_send,
        grad_recv,
    )

    def ahead(i):
        return pltpu.make_async_remote_copy(
            src_ref=outputs.at[i],
            dst_ref=arrived.at[i],
            send_sem=ahead_send.at[i],
            recv_sem=ahead_recv.at[i],
            device_id={"section": after},
        )

    def back(i):
        return pltpu.make_async_remote_copy(
            src_ref=grads_out.at[i],
            dst_ref=grads_in.at[i],
            send_sem=back_send.at[i],
            recv_sem=back_recv.at[i],
            device_id={"section": before},
        )

    def shadow(i):
        return pltpu.make_async_remote_copy(
            src_ref=outputs.at[i],
            dst_ref=shadow_ref.at[i],
            send_sem=shadow_send.at[i],
            recv_sem=shadow_recv.at[i],
            device_id={"section": before},
        )

    def window(owner):
        start = (owner // 2) * (2 * shard) + lax.rem(owner, 2) * (2 * shard - WINDOW)
        return normed_all.at[:, :, pl.ds(pl.multiple_of(start, 128), WINDOW)]

    def unit(step):
        to = lax.rem(mine + step, replicas)
        return pltpu.make_async_remote_copy(
            src_ref=window(to),
            dst_ref=units.at[mine],
            send_sem=unit_send.at[step],
            recv_sem=unit_recv.at[step],
            device_id={"dp": to},
        )

    def columns(k):
        return pl.ds(pl.multiple_of(k * CHUNK, CHUNK), CHUNK)

    def fresh_move(k):
        return pltpu.make_async_remote_copy(
            src_ref=fresh.at[:, columns(k)],
            dst_ref=shadow_weight_ref.at[:, columns(k)],
            send_sem=fresh_send.at[k],
            recv_sem=fresh_recv.at[k],
            device_id={"section": before},
        )

    def flip(k):
        row, column = columns(k // blocks), columns(lax.rem(k, blocks))
        flipped[column, row] = weight[row, column].T

    each(PIECES, *weight_spread)
    loads[0].wait()
    loads[1].start()
    loads[2].start()

    @pl.when(me == 0)
    def _():
        arrived[...] = inputs_ref[...]

    @pl.when(me == sections - 1)
    def _():
        grads_in[...] = cotangent_ref[...]

    @pl.when(me >= sections // 2)
    def _():
        each(blocks * blocks, flip)

    def forward(i):
        @pl.when(me > 0)
        def _():
            ahead(i).wait_recv()

        current = arrived[i].astype(jnp.float32)
        scale = lax.rsqrt(jnp.mean(current * current, axis=-1, keepdims=True) + norm_eps)
        scales[i] = jnp.broadcast_to(scale, (rows, 128))
        normed = (current * scale).astype(jnp.bfloat16)
        normed_all[i] = normed
        for at in range(0, width, CHUNK):
            part = pl.ds(at, CHUNK)
            v = jnp.dot(normed, weight[:, part], preferred_element_type=jnp.float32)
            t = jnp.tanh(tanh_coef * (v + cubic_coef * v * v * v))
            out = arrived[i, :, part].astype(jnp.float32) + branch_scale * (0.5 * v * (1.0 + t))
            outputs[i, :, part] = out.astype(jnp.bfloat16)
            pre_acts[i, :, part] = v
            slope = 0.5 * (1.0 + t) + 0.5 * v * (1.0 - t * t) * tanh_coef * (
                1.0 + 3.0 * cubic_coef * v * v
            )
            slopes[i, :, part] = branch_scale * slope

        @pl.when(me < sections - 1)
        def _():
            ahead(i).start()

        shadow(i).start()

    each(micro, forward)

    def send_units():
        for step in range(1, replicas):
            unit(step).start()
        units[mine] = window(mine)[...]

    def flip_units():
        for step in range(1, replicas):
            unit(step).wait_recv()

        def one(k):
            block = units[k].reshape(tokens, WINDOW)
            units_flipped[:, pl.ds(pl.multiple_of(k * tokens, tokens), tokens)] = block.T

        each(replicas, one)

    @pl.when(me < sections // 2)
    def _():
        each(blocks * blocks, flip)
        send_units()
        flip_units()

    def backward(i):
        @pl.when(me < sections - 1)
        def _():
            back(i).wait_recv()

        grad = grads_in[i].astype(jnp.float32)
        grad_pre = (grad * slopes[i]).astype(jnp.bfloat16)
        gathered[mine, i] = grad_pre

        @pl.when(me > 0)
        def _():
            overlap = jnp.sum(
                grad_pre.astype(jnp.float32) * pre_acts[i], axis=-1, keepdims=True
            ) * (1.0 / width)
            scale = scales[i][:, :1]
            pull = scale * scale * overlap
            for at in range(0, width, CHUNK):
                part = pl.ds(at, CHUNK)
                g = jnp.dot(grad_pre, flipped[:, part], preferred_element_type=jnp.float32)
                a = arrived[i, :, part].astype(jnp.float32)
                total = grads_in[i, :, part].astype(jnp.float32) + scale * g - pull * a
                grads_out[i, :, part] = total.astype(jnp.bfloat16)
            back(i).start()

        grad_spread(i)

        @pl.when((me == 0) & (i > 0))
        def _():
            grad_relay(i - 1)

    each(micro, backward)

    @pl.when(me == 0)
    def _():
        grad_relay(micro - 1)

    @pl.when(me > 0)
    def _():
        each(micro, grad_relay)

    each(micro, grad_cross, grad_finish)

    @pl.when(me >= sections // 2)
    def _():
        send_units()
        flip_units()

    loads[1].wait()
    loads[2].wait()
    skip = lax.rem(mine, 2) * (WINDOW - shard)
    own_rows = mine * shard
    strip = shard // 5

    def step_weights(k):
        part = columns(k)
        grads = gathered[:, :, :, part].reshape(replicas * tokens, CHUNK)
        stage[...] = jnp.dot(units_flipped[...], grads, preferred_element_type=jnp.float32) * (
            1.0 / (replicas * tokens)
        )

        def adam(j):
            here = pl.ds(pl.multiple_of(j * strip, strip), strip)
            gradient = stage[pl.ds(pl.multiple_of(skip + j * strip, 16), strip), :]
            one = beta_one * moment_one[here, part] + (1.0 - beta_one) * gradient
            two = beta_two * moment_two[here, part] + (1.0 - beta_two) * gradient * gradient
            corrected_one = one * (1.0 / (1.0 - beta_one**step_count))
            corrected_two = two * (1.0 / (1.0 - beta_two**step_count))
            direction = corrected_one / (jnp.sqrt(corrected_two) + adam_eps)
            old = weight[pl.ds(pl.multiple_of(own_rows + j * strip, 16), strip), part]
            update_ref[here, part] = direction.astype(jnp.bfloat16)
            fresh[here, part] = (old.astype(jnp.float32) - learn_rate * direction).astype(
                jnp.bfloat16
            )

        each(5, adam)
        fresh_move(k).start()

    each(blocks, step_weights)

    def settle(i):
        @pl.when(me < sections - 1)
        def _():
            ahead(i).wait_send()

        @pl.when(me > 0)
        def _():
            back(i).wait_send()

        shadow(i).wait_send()
        shadow(i).wait_recv()

    def settle_fresh(k):
        fresh_move(k).wait_send()
        fresh_move(k).wait_recv()

    each(micro, settle)
    for step in range(1, replicas):
        unit(step).wait_send()
    each(blocks, settle_fresh)


def on_device(inputs, cotangent, weights, adam_m, adam_v):
    sections = lax.axis_size("section")
    replicas = lax.axis_size("dp")
    tokens, width = inputs.shape
    shard = width // replicas
    rows = tokens // MICRO
    block = (MICRO, rows, width)
    low = jnp.bfloat16
    wide = jnp.float32
    in_vmem = pl.BlockSpec(memory_space=pltpu.VMEM)
    anywhere = pl.BlockSpec(memory_space=pl.ANY)
    dma = pltpu.SemaphoreType.DMA
    update, shadow_weight, shadow_output = pl.pallas_call(
        functools.partial(chain_kernel, sections, replicas),
        out_shape=(
            jax.ShapeDtypeStruct((shard, width), low),
            jax.ShapeDtypeStruct((shard, width), low),
            jax.ShapeDtypeStruct(block, low),
        ),
        in_specs=[in_vmem, in_vmem, anywhere, anywhere, anywhere],
        out_specs=(in_vmem, anywhere, anywhere),
        scratch_shapes=[
            pltpu.VMEM((width, width), low),
            pltpu.VMEM((width, width), low),
            pltpu.VMEM(block, low),
            pltpu.VMEM(block, low),
            pltpu.VMEM(block, low),
            pltpu.VMEM(block, low),
            pltpu.VMEM(block, wide),
            pltpu.VMEM(block, wide),
            pltpu.VMEM((MICRO, rows, 128), wide),
            pltpu.VMEM(block, low),
            pltpu.VMEM((replicas, MICRO, rows, WINDOW), low),
            pltpu.VMEM((WINDOW, replicas * tokens), low),
            pltpu.VMEM((replicas,) + block, low),
            pltpu.VMEM((shard, width), wide),
            pltpu.VMEM((shard, width), wide),
            pltpu.VMEM((shard, width), low),
            pltpu.VMEM((WINDOW, CHUNK), wide),
            dma((3,)),
        ]
        + [dma((MICRO,))] * 6
        + [
            dma((7, PIECES)),
            dma((replicas, PIECES)),
            dma((7, MICRO)),
            dma((replicas, MICRO)),
            dma((replicas,)),
            dma((replicas,)),
            dma((width // CHUNK,)),
            dma((width // CHUNK,)),
        ],
        compiler_params=pltpu.CompilerParams(
            collective_id=0, has_side_effects=True, vmem_limit_bytes=60 * 2**20
        ),
        cost_estimate=pl.CostEstimate(
            flops=6 * tokens * width * width,
            bytes_accessed=16 * shard * width,
            transcendentals=tokens * width,
        ),
    )(
        inputs.reshape(block),
        cotangent.reshape(block),
        weights[0],
        adam_m[0],
        adam_v[0],
    )
    return (update[None], shadow_weight[None], shadow_output.reshape(1, tokens, width))


def solution(mesh):
    in_specs = (
        P("dp", None),
        P("dp", None),
        P("section", "dp", None),
        P("section", "dp", None),
        P("section", "dp", None),
    )
    out_specs = (P("section", "dp", None), P("section", "dp", None), P("section", "dp", None))
    return jax.shard_map(
        on_device, mesh=mesh, in_specs=in_specs, out_specs=out_specs, check_vma=False
    )
```

time: 573 us -> 461 us (0.80)
  waiting for transfers between devices: 235 us -> 0 us
  Pallas kernels: 286 us -> 455 us
  blocking collectives: 21.9 us -> 0 us
  between operations: 14.1 us -> 0.65 us
  matrix products: 8.39 us -> 0 us
    all_gather x2 -> x0, waiting for transfers between devices: 216 us -> none  [the longest x1 161 us: on_device(): full_weight = lax.all_gather(weights[0], 'dp', axis=0, tiled=True)]
    pallas_call x1, Pallas kernels: 286 us -> 455 us  [on_device(): pl.pallas_call(functools.partial(chain_kernel, sections, replicas), out_s...]
    all_to_all x1 -> x0, blocking collectives: 21.9 us -> none  [on_device(): lax.all_to_all(normed, 'dp', split_axis=1, concat_axis=0, tiled=True)]
    ppermute x1 -> x0, waiting for transfers between devices: 18.6 us -> none  [on_device(): shadow_weight = lax.ppermute(new_weight, 'section', shift)]
    dot_general x1 -> x0, matrix products: 8.39 us -> none  [on_device(): lax.dot_general(unit_rows, gathered, (((0,), (0,)), ((), ())), preferred_...]
  transfers between devices with their start and end apart: 3 -> 0, of which waited for: 3 -> 0; matrix products, arithmetic and copies ran while one was open for 0% -> 0% of each run, Pallas kernels for 0% -> 0%
where the time goes in v2:
time: 461 us
  Pallas kernels  455 us (99%)
  local copies, waits for them, and re-layouts  5.2 us (1%)
    pallas_call x1, Pallas kernels, on_device(): pl.pallas_call(functools.partial(chain_kernel, sections, replicas), out_s...  455 us

profile of v2, /device:TPU:4, one launch (start us, length us, event | category | flops | bytes accessed | tf_op | source)
XLA Modules:
  0.0 461.0 jit_solution(9698931416363612090)
XLA Ops:
  0.6 455.1 %shard_map.76 = (bf16[320,2560]{1,0:T(8,128)(2,1)}, bf16[320,2560]{1,0:T(8,128)(2,1)}, bf16[8,16,2560]{2,1,0:T(8,128)(2,1)}) custom-call(bf16[8,16,2560]{2,1,0:T(8,128)(2,1)} %bitcast.14, bf16[8,16,2560]{2,1,0:T(8,128)(2,1)} %bitcast.15, bf16[320,2560]{1,0:T(8,128)(2,1)} %bitcast.13, f32[320,2560]{1,0:T(8,128)} %bitcast.11, f32[320,2560]{1,0:T(8,128)} %bitcast.12), custom_call_target="tpu_custom_call" | custom-call | flops 5033164800 | bytes 13107200 | tf_op jit(solution)/shard_map/pallas_call | solution.py:406
  455.8 0.0 copy-start
  455.8 2.8 copy.11
  458.6 0.0 copy-done
  458.6 0.0 copy-start.1
  458.6 1.2 copy.12
  459.8 0.4 copy-done.1
  460.1 0.8 copy.13
Async XLA Ops:
  455.8 2.8 copy-start
  458.6 1.5 copy-start.1

commit v3 on v2

--- a/solution.py
+++ b/solution.py
@@ -8,6 +8,8 @@
 
 MICRO = 8
 CHUNK = 256
+PART = 512
+APART = 2
 PIECES = 4
 WINDOW = 384
 
@@ -50,6 +52,7 @@
     moment_two,
     fresh,
     stage,
+    sums,
     load_sem,
     ahead_send,
     ahead_recv,
@@ -65,6 +68,9 @@
     unit_recv,
     fresh_send,
     fresh_recv,
+    part_send,
+    part_recv,
+    passed,
 ):
     micro, rows, width = arrived.shape
     shard = width // replicas
@@ -72,6 +78,7 @@
     ring = replicas // 2
     tokens = micro * rows
     blocks = width // CHUNK
+    pairs = micro // 2
     me = lax.axis_index("section")
     mine = lax.axis_index("dp")
     after = lax.rem(me + 1, sections)
@@ -94,13 +101,15 @@
     ]
     loads[0].start()
     barrier = pltpu.get_barrier_semaphore()
-    for other in (before, after):
+    later = lax.rem(me + APART, sections)
+    earlier = lax.rem(me + sections - APART, sections)
+    for other in (before, after, earlier, later):
         pl.semaphore_signal(barrier, inc=1, device_id={"section": other})
     for step in range(1, replicas):
         pl.semaphore_signal(barrier, inc=1, device_id={"dp": lax.rem(mine + step, replicas)})
-    pl.semaphore_wait(barrier, replicas + 1)
-
-    def spread_over(place, own, sends, recvs):
+    pl.semaphore_wait(barrier, replicas + 3)
+
+    def spread_over(place, own, sends, recvs, crosses):
         def move(lane, owner, i, to, source=None):
             return pltpu.make_async_remote_copy(
                 src_ref=place(owner, i) if source is None else source,
@@ -113,41 +122,64 @@
         def landed(owner, i):
             move(0, owner, i, mine).wait_recv()
 
-        def spread(i):
-            for lane, to in enumerate((facing, right, left)):
-                move(lane, mine, i, to, own(i)).start()
-
-        def relay(i):
+        def spread_line(i):
+            move(1, mine, i, right, own(i)).start()
+            move(2, mine, i, left, own(i)).start()
+
+        def spread_face(i):
+            move(0, mine, i, facing, own(i)).start()
+
+        def pass_on(i):
             turn = 2 * lax.rem(i, 2) - 1
             landed(peer(turn), i)
             move(3, peer(turn), i, peer(-turn)).start()
+
+        def relay(i):
             landed(facing, i)
             move(4, facing, i, right).start()
             move(5, facing, i, left).start()
 
         def cross(i):
-            landed(far, i)
-            move(6, far, i, facing).start()
+            turn = 2 * lax.rem(i, 2) - 1
+
+            @pl.when(crosses(i))
+            def _():
+                landed(far, i)
+                move(6, far, i, facing).start()
+
+            @pl.when(jnp.logical_not(crosses(i)))
+            def _():
+                landed(peer(turn, True), i)
+                move(6, peer(turn, True), i, peer(-turn)).start()
 
         def finish(i):
             turn = 2 * lax.rem(i, 2) - 1
             landed(peer(-turn), i)
-            landed(peer(1, True), i)
-            landed(peer(-1, True), i)
+            landed(peer(-turn, True), i)
             landed(peer(2, True), i)
+
+            @pl.when(crosses(i))
+            def _():
+                landed(peer(turn, True), i)
+
+            @pl.when(jnp.logical_not(crosses(i)))
+            def _():
+                landed(far, i)
+
+        def sent(i):
             for lane in range(7):
                 move(lane, mine, i, mine).wait_send()
 
-        return spread, relay, cross, finish
-
-    def each(count, *steps):
+        return spread_line, spread_face, pass_on, relay, cross, finish, sent
+
+    def each(count, *steps, first=0):
         for step in steps:
 
             def one(i, carry, step=step):
                 step(i)
                 return carry
 
-            lax.fori_loop(0, count, one, 0)
+            lax.fori_loop(first, first + count, one, 0)
 
     def weight_place(owner, i):
         return weight.at[pl.ds(pl.multiple_of(owner * shard + i * piece, 16), piece)]
@@ -157,12 +189,28 @@
         lambda i: shard_ref.at[pl.ds(pl.multiple_of(i * piece, 16), piece)],
         weight_send,
         weight_recv,
+        lambda i: i >= 0,
     )
-    grad_spread, grad_relay, grad_cross, grad_finish = spread_over(
-        lambda owner, i: gathered.at[owner, i],
-        lambda i: gathered.at[mine, i],
+
+    def grad_place(owner, i):
+        pair = pl.ds(2 * lax.rem(i, pairs), 2)
+        half = pl.ds(pl.multiple_of((i // pairs) * (width // 2), 128), width // 2)
+        return gathered.at[owner, pair, :, half]
+
+    (
+        grad_line,
+        grad_face,
+        grad_pass,
+        grad_relay,
+        grad_cross,
+        grad_finish,
+        grad_sent,
+    ) = spread_over(
+        grad_place,
+        lambda i: grad_place(mine, i),
         grad_send,
         grad_recv,
+        lambda i: (me < 2) | (lax.rem(i // 2, 2) == 0),
     )
 
     def ahead(i):
@@ -174,12 +222,32 @@
             device_id={"section": after},
         )
 
+    def ahead_part(i, k):
+        part = pl.ds(k * PART, PART)
+        return pltpu.make_async_remote_copy(
+            src_ref=outputs.at[i, :, part],
+            dst_ref=arrived.at[i, :, part],
+            send_sem=part_send.at[0, i, k],
+            recv_sem=part_recv.at[0, i, k],
+            device_id={"section": after},
+        )
+
     def back(i):
         return pltpu.make_async_remote_copy(
             src_ref=grads_out.at[i],
             dst_ref=grads_in.at[i],
             send_sem=back_send.at[i],
             recv_sem=back_recv.at[i],
+            device_id={"section": before},
+        )
+
+    def back_part(i, k):
+        part = pl.ds(k * PART, PART)
+        return pltpu.make_async_remote_copy(
+            src_ref=grads_out.at[i, :, part],
+            dst_ref=grads_in.at[i, :, part],
+            send_sem=part_send.at[1, i, k],
+            recv_sem=part_recv.at[1, i, k],
             device_id={"section": before},
         )
 
@@ -239,35 +307,87 @@
     def _():
         each(blocks * blocks, flip)
 
-    def forward(i):
-        @pl.when(me > 0)
-        def _():
-            ahead(i).wait_recv()
-
+    def keep(i, at, v, t):
+        part = pl.ds(at, PART)
+        pre_acts[i, :, part] = v
+        slope = 0.5 * (1.0 + t) + 0.5 * v * (1.0 - t * t) * tanh_coef * (
+            1.0 + 3.0 * cubic_coef * v * v
+        )
+        slopes[i, :, part] = branch_scale * slope
+
+    def finish_output(i, at, v):
+        part = pl.ds(at, PART)
+        t = jnp.tanh(tanh_coef * (v + cubic_coef * v * v * v))
+        out = arrived[i, :, part].astype(jnp.float32) + branch_scale * (0.5 * v * (1.0 + t))
+        outputs[i, :, part] = out.astype(jnp.bfloat16)
+        return t
+
+    def rms_scale(squares):
+        return lax.rsqrt(squares * (1.0 / width) + norm_eps)
+
+    def forward_spread(i):
+        ahead(i).wait_recv()
         current = arrived[i].astype(jnp.float32)
-        scale = lax.rsqrt(jnp.mean(current * current, axis=-1, keepdims=True) + norm_eps)
+        scale = rms_scale(jnp.sum(current * current, axis=-1, keepdims=True))
+        raw = arrived[i]
+
+        def product(at):
+            return jnp.dot(raw, weight[:, pl.ds(at, PART)], preferred_element_type=jnp.float32)
+
+        following = product(0)
+        for at in range(0, width, PART):
+            v = following * scale
+            if at + PART < width:
+                following = product(at + PART)
+            t = finish_output(i, at, v)
+
+            @pl.when(me < sections - 1)
+            def _():
+                ahead_part(i, at // PART).start()
+
+            keep(i, at, v, t)
         scales[i] = jnp.broadcast_to(scale, (rows, 128))
-        normed = (current * scale).astype(jnp.bfloat16)
-        normed_all[i] = normed
-        for at in range(0, width, CHUNK):
-            part = pl.ds(at, CHUNK)
-            v = jnp.dot(normed, weight[:, part], preferred_element_type=jnp.float32)
-            t = jnp.tanh(tanh_coef * (v + cubic_coef * v * v * v))
-            out = arrived[i, :, part].astype(jnp.float32) + branch_scale * (0.5 * v * (1.0 + t))
-            outputs[i, :, part] = out.astype(jnp.bfloat16)
-            pre_acts[i, :, part] = v
-            slope = 0.5 * (1.0 + t) + 0.5 * v * (1.0 - t * t) * tanh_coef * (
-                1.0 + 3.0 * cubic_coef * v * v
-            )
-            slopes[i, :, part] = branch_scale * slope
-
-        @pl.when(me < sections - 1)
-        def _():
-            ahead(i).start()
-
+        normed_all[i] = (current * scale).astype(jnp.bfloat16)
         shadow(i).start()
 
-    each(micro, forward)
+    def forward_collect(i):
+        squares = jnp.zeros((rows, 1), jnp.float32)
+        for at in range(0, width, PART):
+            part = pl.ds(at, PART)
+
+            @pl.when(me > 0)
+            def _():
+                ahead_part(i, at // PART).wait_recv()
+
+            raw = arrived[i, :, part]
+            current = raw.astype(jnp.float32)
+            squares += jnp.sum(current * current, axis=-1, keepdims=True)
+            product = jnp.dot(raw, weight[part, :], preferred_element_type=jnp.float32)
+            if at == 0:
+                sums[...] = product
+            else:
+                sums[...] += product
+        scale = rms_scale(squares)
+        values = []
+        for at in range(0, width, PART):
+            v = sums[:, pl.ds(at, PART)] * scale
+            values.append((at, v, finish_output(i, at, v)))
+        ahead(i).start()
+        shadow(i).start()
+        for at, v, t in values:
+            keep(i, at, v, t)
+        scales[i] = jnp.broadcast_to(scale, (rows, 128))
+        normed_all[i] = (arrived[i].astype(jnp.float32) * scale).astype(jnp.bfloat16)
+
+    odd = lax.rem(me, 2)
+
+    @pl.when(odd == 1)
+    def _():
+        each(micro, forward_spread)
+
+    @pl.when(odd == 0)
+    def _():
+        each(micro, forward_collect)
 
     def send_units():
         for step in range(1, replicas):
@@ -290,13 +410,25 @@
         send_units()
         flip_units()
 
-    def backward(i):
-        @pl.when(me < sections - 1)
+    def finish_grad(i, at, g, scale, pull):
+        part = pl.ds(at, PART)
+        a = arrived[i, :, part].astype(jnp.float32)
+        total = grads_in[i, :, part].astype(jnp.float32) + scale * g - pull * a
+        grads_out[i, :, part] = total.astype(jnp.bfloat16)
+
+    def push_grads(i):
+        @pl.when(lax.rem(i, 2) == 1)
         def _():
-            back(i).wait_recv()
-
-        grad = grads_in[i].astype(jnp.float32)
-        grad_pre = (grad * slopes[i]).astype(jnp.bfloat16)
+            for half in range(2):
+                grad_line(half * pairs + i // 2)
+
+                @pl.when(me < 2)
+                def _(half=half):
+                    grad_face(half * pairs + i // 2)
+
+    def backward_spread(i):
+        back(i).wait_recv()
+        grad_pre = (grads_in[i].astype(jnp.float32) * slopes[i]).astype(jnp.bfloat16)
         gathered[mine, i] = grad_pre
 
         @pl.when(me > 0)
@@ -306,31 +438,70 @@
             ) * (1.0 / width)
             scale = scales[i][:, :1]
             pull = scale * scale * overlap
-            for at in range(0, width, CHUNK):
-                part = pl.ds(at, CHUNK)
-                g = jnp.dot(grad_pre, flipped[:, part], preferred_element_type=jnp.float32)
-                a = arrived[i, :, part].astype(jnp.float32)
-                total = grads_in[i, :, part].astype(jnp.float32) + scale * g - pull * a
-                grads_out[i, :, part] = total.astype(jnp.bfloat16)
-            back(i).start()
-
-        grad_spread(i)
-
-        @pl.when((me == 0) & (i > 0))
-        def _():
-            grad_relay(i - 1)
-
-    each(micro, backward)
-
-    @pl.when(me == 0)
-    def _():
-        grad_relay(micro - 1)
-
-    @pl.when(me > 0)
-    def _():
-        each(micro, grad_relay)
-
-    each(micro, grad_cross, grad_finish)
+
+            def product(at):
+                return jnp.dot(
+                    grad_pre, flipped[:, pl.ds(at, PART)], preferred_element_type=jnp.float32
+                )
+
+            following = product(0)
+            for at in range(0, width, PART):
+                g = following
+                if at + PART < width:
+                    following = product(at + PART)
+                finish_grad(i, at, g, scale, pull)
+                back_part(i, at // PART).start()
+        push_grads(i)
+
+    def backward_collect(i):
+        overlap = jnp.zeros((rows, 1), jnp.float32)
+        for at in range(0, width, PART):
+            part = pl.ds(at, PART)
+
+            @pl.when(me < sections - 1)
+            def _():
+                back_part(i, at // PART).wait_recv()
+
+            grad_pre = (grads_in[i, :, part].astype(jnp.float32) * slopes[i, :, part]).astype(
+                jnp.bfloat16
+            )
+            gathered[mine, i, :, part] = grad_pre
+            overlap += jnp.sum(
+                grad_pre.astype(jnp.float32) * pre_acts[i, :, part], axis=-1, keepdims=True
+            )
+            product = jnp.dot(grad_pre, flipped[part, :], preferred_element_type=jnp.float32)
+            if at == 0:
+                sums[...] = product
+            else:
+                sums[...] += product
+        scale = scales[i][:, :1]
+        pull = scale * scale * overlap * (1.0 / width)
+        for at in range(0, width, PART):
+            finish_grad(i, at, sums[:, pl.ds(at, PART)], scale, pull)
+        back(i).start()
+        push_grads(i)
+
+    @pl.when(odd == 0)
+    def _():
+        each(micro, backward_spread)
+
+    @pl.when(odd == 1)
+    def _():
+        each(micro, backward_collect)
+
+    @pl.when((me > 0) & (me < sections - APART))
+    def _():
+        pl.semaphore_signal(passed, inc=1, device_id={"section": later})
+
+    @pl.when(me > APART)
+    def _():
+        pl.semaphore_wait(passed, 1)
+
+    @pl.when(me >= 2)
+    def _():
+        each(micro, grad_face)
+
+    each(micro, grad_pass, grad_relay, grad_cross)
 
     @pl.when(me >= sections // 2)
     def _():
@@ -367,16 +538,28 @@
         each(5, adam)
         fresh_move(k).start()
 
-    each(blocks, step_weights)
+    for half in range(2):
+        each(pairs, grad_finish, first=half * pairs)
+        each(blocks // 2, step_weights, first=half * (blocks // 2))
 
     def settle(i):
-        @pl.when(me < sections - 1)
+        @pl.when(odd == 0)
         def _():
             ahead(i).wait_send()
 
-        @pl.when(me > 0)
+        @pl.when(odd == 1)
         def _():
             back(i).wait_send()
+
+        for k in range(width // PART):
+
+            @pl.when((odd == 1) & (me < sections - 1))
+            def _(k=k):
+                ahead_part(i, k).wait_send()
+
+            @pl.when((odd == 0) & (me > 0))
+            def _(k=k):
+                back_part(i, k).wait_send()
 
         shadow(i).wait_send()
         shadow(i).wait_recv()
@@ -385,7 +568,7 @@
         fresh_move(k).wait_send()
         fresh_move(k).wait_recv()
 
-    each(micro, settle)
+    each(micro, settle, grad_sent)
     for step in range(1, replicas):
         unit(step).wait_send()
     each(blocks, settle_fresh)
@@ -430,6 +613,7 @@
             pltpu.VMEM((shard, width), wide),
             pltpu.VMEM((shard, width), low),
             pltpu.VMEM((WINDOW, CHUNK), wide),
+            pltpu.VMEM((rows, width), wide),
             dma((3,)),
         ]
         + [dma((MICRO,))] * 6
@@ -442,6 +626,9 @@
             dma((replicas,)),
             dma((width // CHUNK,)),
             dma((width // CHUNK,)),
+            dma((2, MICRO, width // PART)),
+            dma((2, MICRO, width // PART)),
+            pltpu.SemaphoreType.REGULAR,
         ],
         compiler_params=pltpu.CompilerParams(
             collective_id=0, has_side_effects=True, vmem_limit_bytes=60 * 2**20

time: 461 us -> 390 us (0.85); the launches traced: 461 us -> 384 us
  Pallas kernels: 455 us -> 379 us
    pallas_call x1, Pallas kernels: 455 us -> 379 us  [on_device(): pl.pallas_call(functools.partial(chain_kernel, sections, replicas), out_s...]
where the time goes in v3:
time: 390 us; the launch traced here: 384 us
  Pallas kernels  379 us (97%)
  local copies, waits for them, and re-layouts  5.2 us (1%)
    pallas_call x1, Pallas kernels, on_device(): pl.pallas_call(functools.partial(chain_kernel, sections, replicas), out_s...  379 us

profile of v3, /device:TPU:4, one launch (start us, length us, event | category | flops | bytes accessed | tf_op | source)
XLA Modules:
  0.0 384.4 jit_solution(14913223265886799630)
XLA Ops:
  0.6 378.6 %shard_map.76 = (bf16[320,2560]{1,0:T(8,128)(2,1)}, bf16[320,2560]{1,0:T(8,128)(2,1)}, bf16[8,16,2560]{2,1,0:T(8,128)(2,1)}) custom-call(bf16[8,16,2560]{2,1,0:T(8,128)(2,1)} %bitcast.14, bf16[8,16,2560]{2,1,0:T(8,128)(2,1)} %bitcast.15, bf16[320,2560]{1,0:T(8,128)(2,1)} %bitcast.13, f32[320,2560]{1,0:T(8,128)} %bitcast.11, f32[320,2560]{1,0:T(8,128)} %bitcast.12), custom_call_target="tpu_custom_call" | custom-call | flops 5033164800 | bytes 13107200 | tf_op jit(solution)/shard_map/pallas_call | solution.py:589
  379.2 0.0 copy-start
  379.2 2.8 copy.11
  382.0 0.0 copy-done
  382.0 0.0 copy-start.1
  382.0 1.2 copy.12
  383.2 0.4 copy-done.1
  383.6 0.8 copy.13
Async XLA Ops:
  379.2 2.8 copy-start
  382.0 1.5 copy-start.1

commit v4 on v3

--- a/solution.py
+++ b/solution.py
@@ -325,55 +325,73 @@
     def rms_scale(squares):
         return lax.rsqrt(squares * (1.0 / width) + norm_eps)
 
-    def forward_spread(i):
+    def lanes(values):
+        total = values[:, :128]
+        for at in range(128, values.shape[1], 128):
+            total += values[:, at : at + 128]
+        return total
+
+    def row_total(partial):
+        return jnp.sum(partial, axis=-1, keepdims=True)
+
+    def forward_spread(last, i):
         ahead(i).wait_recv()
-        current = arrived[i].astype(jnp.float32)
-        scale = rms_scale(jnp.sum(current * current, axis=-1, keepdims=True))
         raw = arrived[i]
 
         def product(at):
             return jnp.dot(raw, weight[:, pl.ds(at, PART)], preferred_element_type=jnp.float32)
 
+        following = product(0)
+        current = raw.astype(jnp.float32)
+        scale = rms_scale(row_total(lanes(current * current)))
+        scales[i] = jnp.broadcast_to(scale, (rows, 128))
+        for at in range(0, width, PART):
+            v = following * scale
+            if at + PART < width:
+                following = product(at + PART)
+            t = finish_output(i, at, v)
+            if at + PART < width:
+                keep(i, at, v, t)
+            if not last:
+                ahead_part(i, at // PART).start()
+        keep(i, at, v, t)
+        normed_all[i] = (arrived[i].astype(jnp.float32) * scale).astype(jnp.bfloat16)
+
+    def forward_collect(first, i):
+        squares = jnp.zeros((rows, 128), jnp.float32)
+        for at in range(0, width - PART, PART):
+            part = pl.ds(at, PART)
+            if not first:
+                ahead_part(i, at // PART).wait_recv()
+            raw = arrived[i, :, part]
+            current = raw.astype(jnp.float32)
+            squares += lanes(current * current)
+            product = jnp.dot(raw, weight[part, :], preferred_element_type=jnp.float32)
+            if at == 0:
+                sums[...] = product
+            else:
+                sums[...] += product
+        end = pl.ds(width - PART, PART)
+        if not first:
+            ahead_part(i, width // PART - 1).wait_recv()
+        raw = arrived[i, :, end]
+
+        def product(at):
+            part = pl.ds(at, PART)
+            return sums[:, part] + jnp.dot(
+                raw, weight[end, part], preferred_element_type=jnp.float32
+            )
+
+        current = raw.astype(jnp.float32)
+        scale = rms_scale(row_total(squares + lanes(current * current)))
+        values = []
         following = product(0)
         for at in range(0, width, PART):
             v = following * scale
             if at + PART < width:
                 following = product(at + PART)
-            t = finish_output(i, at, v)
-
-            @pl.when(me < sections - 1)
-            def _():
-                ahead_part(i, at // PART).start()
-
-            keep(i, at, v, t)
-        scales[i] = jnp.broadcast_to(scale, (rows, 128))
-        normed_all[i] = (current * scale).astype(jnp.bfloat16)
-        shadow(i).start()
-
-    def forward_collect(i):
-        squares = jnp.zeros((rows, 1), jnp.float32)
-        for at in range(0, width, PART):
-            part = pl.ds(at, PART)
-
-            @pl.when(me > 0)
-            def _():
-                ahead_part(i, at // PART).wait_recv()
-
-            raw = arrived[i, :, part]
-            current = raw.astype(jnp.float32)
-            squares += jnp.sum(current * current, axis=-1, keepdims=True)
-            product = jnp.dot(raw, weight[part, :], preferred_element_type=jnp.float32)
-            if at == 0:
-                sums[...] = product
-            else:
-                sums[...] += product
-        scale = rms_scale(squares)
-        values = []
-        for at in range(0, width, PART):
-            v = sums[:, pl.ds(at, PART)] * scale
             values.append((at, v, finish_output(i, at, v)))
         ahead(i).start()
-        shadow(i).start()
         for at, v, t in values:
             keep(i, at, v, t)
         scales[i] = jnp.broadcast_to(scale, (rows, 128))
@@ -381,13 +399,21 @@
 
     odd = lax.rem(me, 2)
 
-    @pl.when(odd == 1)
-    def _():
-        each(micro, forward_spread)
-
-    @pl.when(odd == 0)
-    def _():
-        each(micro, forward_collect)
+    @pl.when((odd == 1) & (me < sections - 1))
+    def _():
+        each(micro, functools.partial(forward_spread, False))
+
+    @pl.when(me == sections - 1)
+    def _():
+        each(micro, functools.partial(forward_spread, True))
+
+    @pl.when((odd == 0) & (me > 0))
+    def _():
+        each(micro, functools.partial(forward_collect, False))
+
+    @pl.when(me == 0)
+    def _():
+        each(micro, functools.partial(forward_collect, True))
 
     def send_units():
         for step in range(1, replicas):
@@ -406,6 +432,7 @@
 
     @pl.when(me < sections // 2)
     def _():
+        each(micro, lambda i: shadow(i).start())
         each(blocks * blocks, flip)
         send_units()
         flip_units()
@@ -453,31 +480,46 @@
                 back_part(i, at // PART).start()
         push_grads(i)
 
-    def backward_collect(i):
-        overlap = jnp.zeros((rows, 1), jnp.float32)
-        for at in range(0, width, PART):
+    def backward_collect(first, i):
+        overlap = jnp.zeros((rows, 128), jnp.float32)
+
+        def grad_part(at):
             part = pl.ds(at, PART)
-
-            @pl.when(me < sections - 1)
-            def _():
+            if not first:
                 back_part(i, at // PART).wait_recv()
-
             grad_pre = (grads_in[i, :, part].astype(jnp.float32) * slopes[i, :, part]).astype(
                 jnp.bfloat16
             )
             gathered[mine, i, :, part] = grad_pre
-            overlap += jnp.sum(
-                grad_pre.astype(jnp.float32) * pre_acts[i, :, part], axis=-1, keepdims=True
+            return grad_pre, lanes(grad_pre.astype(jnp.float32) * pre_acts[i, :, part])
+
+        for at in range(0, width - PART, PART):
+            grad_pre, extra = grad_part(at)
+            overlap += extra
+            product = jnp.dot(
+                grad_pre, flipped[pl.ds(at, PART), :], preferred_element_type=jnp.float32
             )
-            product = jnp.dot(grad_pre, flipped[part, :], preferred_element_type=jnp.float32)
             if at == 0:
                 sums[...] = product
             else:
                 sums[...] += product
+        grad_pre, extra = grad_part(width - PART)
+        end = pl.ds(width - PART, PART)
+
+        def finish_product(at):
+            part = pl.ds(at, PART)
+            return sums[:, part] + jnp.dot(
+                grad_pre, flipped[end, part], preferred_element_type=jnp.float32
+            )
+
+        following = finish_product(0)
         scale = scales[i][:, :1]
-        pull = scale * scale * overlap * (1.0 / width)
+        pull = scale * scale * row_total(overlap + extra) * (1.0 / width)
         for at in range(0, width, PART):
-            finish_grad(i, at, sums[:, pl.ds(at, PART)], scale, pull)
+            g = following
+            if at + PART < width:
+                following = finish_product(at + PART)
+            finish_grad(i, at, g, scale, pull)
         back(i).start()
         push_grads(i)
 
@@ -485,9 +527,13 @@
     def _():
         each(micro, backward_spread)
 
-    @pl.when(odd == 1)
-    def _():
-        each(micro, backward_collect)
+    @pl.when((odd == 1) & (me < sections - 1))
+    def _():
+        each(micro, functools.partial(backward_collect, False))
+
+    @pl.when(me == sections - 1)
+    def _():
+        each(micro, functools.partial(backward_collect, True))
 
     @pl.when((me > 0) & (me < sections - APART))
     def _():
@@ -505,6 +551,7 @@
 
     @pl.when(me >= sections // 2)
     def _():
+        each(micro, lambda i: shadow(i).start())
         send_units()
         flip_units()
 

time: 390 us -> 381 us (0.977)
  Pallas kernels: 379 us -> 369 us
    pallas_call x1, Pallas kernels: 379 us -> 369 us  [on_device(): pl.pallas_call(functools.partial(chain_kernel, sections, replicas), out_s...]
where the time goes in v4:
time: 381 us; the launch traced here: 375 us
  Pallas kernels  369 us (97%)
  local copies, waits for them, and re-layouts  5.2 us (1%)
    pallas_call x1, Pallas kernels, on_device(): pl.pallas_call(functools.partial(chain_kernel, sections, replicas), out_s...  369 us

profile of v4, /device:TPU:4, one launch (start us, length us, event | category | flops | bytes accessed | tf_op | source)
XLA Modules:
  0.0 374.6 jit_solution(15149041701292530374)
XLA Ops:
  0.6 368.8 %shard_map.76 = (bf16[320,2560]{1,0:T(8,128)(2,1)}, bf16[320,2560]{1,0:T(8,128)(2,1)}, bf16[8,16,2560]{2,1,0:T(8,128)(2,1)}) custom-call(bf16[8,16,2560]{2,1,0:T(8,128)(2,1)} %bitcast.14, bf16[8,16,2560]{2,1,0:T(8,128)(2,1)} %bitcast.15, bf16[320,2560]{1,0:T(8,128)(2,1)} %bitcast.13, f32[320,2560]{1,0:T(8,128)} %bitcast.11, f32[320,2560]{1,0:T(8,128)} %bitcast.12), custom_call_target="tpu_custom_call" | custom-call | flops 5033164800 | bytes 13107200 | tf_op jit(solution)/shard_map/pallas_call | solution.py:636
  369.4 0.0 copy-start
  369.4 2.8 copy.11
  372.2 0.0 copy-done
  372.2 0.0 copy-start.1
  372.2 1.2 copy.12
  373.4 0.4 copy-done.1
  373.8 0.8 copy.13
Async XLA Ops:
  369.4 2.8 copy-start
  372.2 1.5 copy-start.1

commit v5 on v4

--- a/solution.py
+++ b/solution.py
@@ -10,7 +10,9 @@
 CHUNK = 256
 PART = 512
 APART = 2
-PIECES = 4
+EARLY = 2
+PIECES = 10
+SHIFTED = 1
 WINDOW = 384
 
 branch_scale = 0.5
@@ -109,7 +111,7 @@
         pl.semaphore_signal(barrier, inc=1, device_id={"dp": lax.rem(mine + step, replicas)})
     pl.semaphore_wait(barrier, replicas + 3)
 
-    def spread_over(place, own, sends, recvs, crosses):
+    def spread_over(place, own, sends, recvs, crosses, shifted):
         def move(lane, owner, i, to, source=None):
             return pltpu.make_async_remote_copy(
                 src_ref=place(owner, i) if source is None else source,
@@ -135,9 +137,19 @@
             move(3, peer(turn), i, peer(-turn)).start()
 
         def relay(i):
+            turn = 2 * lax.rem(i, 2) - 1
             landed(facing, i)
-            move(4, facing, i, right).start()
-            move(5, facing, i, left).start()
+
+            @pl.when(i >= shifted)
+            def _():
+                move(4, facing, i, right).start()
+                move(5, facing, i, left).start()
+
+            @pl.when(i < shifted)
+            def _():
+                landed(peer(-turn), i)
+                move(4, peer(turn), i, facing).start()
+                move(5, peer(-turn), i, facing).start()
 
         def cross(i):
             turn = 2 * lax.rem(i, 2) - 1
@@ -154,7 +166,11 @@
 
         def finish(i):
             turn = 2 * lax.rem(i, 2) - 1
-            landed(peer(-turn), i)
+
+            @pl.when(i >= shifted)
+            def _():
+                landed(peer(-turn), i)
+
             landed(peer(-turn, True), i)
             landed(peer(2, True), i)
 
@@ -190,6 +206,7 @@
         weight_send,
         weight_recv,
         lambda i: i >= 0,
+        SHIFTED,
     )
 
     def grad_place(owner, i):
@@ -211,6 +228,7 @@
         grad_send,
         grad_recv,
         lambda i: (me < 2) | (lax.rem(i // 2, 2) == 0),
+        0,
     )
 
     def ahead(i):
@@ -290,7 +308,8 @@
         row, column = columns(k // blocks), columns(lax.rem(k, blocks))
         flipped[column, row] = weight[row, column].T
 
-    each(PIECES, *weight_spread)
+    *weight_steps, weight_sent = weight_spread
+    each(PIECES, *weight_steps)
     loads[0].wait()
     loads[1].start()
     loads[2].start()
@@ -449,7 +468,7 @@
             for half in range(2):
                 grad_line(half * pairs + i // 2)
 
-                @pl.when(me < 2)
+                @pl.when(me < EARLY)
                 def _(half=half):
                     grad_face(half * pairs + i // 2)
 
@@ -543,7 +562,7 @@
     def _():
         pl.semaphore_wait(passed, 1)
 
-    @pl.when(me >= 2)
+    @pl.when(me >= EARLY)
     def _():
         each(micro, grad_face)
 
@@ -615,6 +634,7 @@
         fresh_move(k).wait_send()
         fresh_move(k).wait_recv()
 
+    each(PIECES, weight_sent)
     each(micro, settle, grad_sent)
     for step in range(1, replicas):
         unit(step).wait_send()

time: 381 us -> 378 us (level)
  no operation moved by 1% of the time
where the time goes in v5:
time: 378 us; the launch traced here: 372 us
  Pallas kernels  366 us (97%)
  local copies, waits for them, and re-layouts  5.2 us (1%)
    pallas_call x1, Pallas kernels, on_device(): pl.pallas_call(functools.partial(chain_kernel, sections, replicas), out_s...  366 us

profile of v5, /device:TPU:4, one launch (start us, length us, event | category | flops | bytes accessed | tf_op | source)
XLA Modules:
  0.0 371.9 jit_solution(12831802552503764033)
XLA Ops:
  0.6 366.0 %shard_map.76 = (bf16[320,2560]{1,0:T(8,128)(2,1)}, bf16[320,2560]{1,0:T(8,128)(2,1)}, bf16[8,16,2560]{2,1,0:T(8,128)(2,1)}) custom-call(bf16[8,16,2560]{2,1,0:T(8,128)(2,1)} %bitcast.14, bf16[8,16,2560]{2,1,0:T(8,128)(2,1)} %bitcast.15, bf16[320,2560]{1,0:T(8,128)(2,1)} %bitcast.13, f32[320,2560]{1,0:T(8,128)} %bitcast.11, f32[320,2560]{1,0:T(8,128)} %bitcast.12), custom_call_target="tpu_custom_call" | custom-call | flops 5033164800 | bytes 13107200 | tf_op jit(solution)/shard_map/pallas_call | solution.py:656
  366.6 0.0 copy-start
  366.7 2.8 copy.11
  369.5 0.0 copy-done
  369.5 0.0 copy-start.1
  369.5 1.2 copy.12
  370.6 0.4 copy-done.1
  371.0 0.8 copy.13
Async XLA Ops:
  366.6 2.8 copy-start
  369.5 1.5 copy-start.1
